TPU v7x, 32 devices: a whole 2x2x4 slice. The times are simulated.
32 devices in a mesh: head: 8 (over z, y), kdim: 4 (over x, core).
Axes of the slice: x: 2, y: 2, z: 4, core: 2. Of those that a mesh axis runs over, the one named last changes fastest.
Arguments:
- hidden: bfloat16 [3, 1024, 8192], P(None, None, 'kdim'), may hold values from -6 to 6
- joined_weight: bfloat16 [3, 8192, 10240], P(None, 'kdim', 'head'), may hold values from -0.0625 to 0.0625
- src_block: int32 [8], replicated, may hold values from 0 to 7, each once
- group_map: int32 [8], replicated, may hold values from 0 to 7, each once
- q_slot: int32 [64], replicated, may hold values from 0 to 7, as said below
Outputs:
- qkv: float32 [3, 1024, 10240], P(None, 'kdim', 'head')
Inputs may be any that keep to these rules, and one draw needn't show every extreme that they name: `q_slot`: for every key head g, the entries g * 8 to g * 8 + 7 are a permutation of 0 to 7.
All inputs are finite; a program needn't handle non-finite values.
Results may differ from a plain program's by a relative error of at most 0.0003.
Values may be sent and summed in bfloat16 or wider, within the bound.
A program may use at most 128 MiB of HBM per device.

v0:
```python
import jax
import jax.numpy as jnp
from jax import lax
from jax.sharding import PartitionSpec as P

HEAD_DIM = 128
Q_HEADS = 64
KV_HEADS = 8
GROUP = 8


def from_partner(block, axis, stride):
    count = lax.axis_size(axis)
    route = []
    for low in range(count):
        high = low | 1 << stride
        if high != low and high < count:
            route += [(low, high), (high, low)]
    return lax.ppermute(block, axis, route)


def lookup(table, where_at):
    entries = jnp.arange(table.shape[0], dtype=jnp.int32)
    return jnp.sum(table[None, :] * (entries[None, :] == where_at[:, None]), axis=1)


def regroup(
    payload,
    start_keys,
    position,
    quarter,
    head_index,
    group_slots,
    slot_count,
    low_bits,
    sort_bits,
    pair_swap,
    part_swap,
):
    places = jnp.arange(KV_HEADS, dtype=jnp.int32)
    key_list = start_keys
    for level in range(1, sort_bits + 1):
        for stride in reversed(range(level)):
            partner = pair_swap(payload, low_bits + stride)
            partner_places = jnp.bitwise_xor(places, 1 << stride)
            partner_keys = lookup(key_list, partner_places)
            upper_half = jnp.bitwise_and(jnp.right_shift(places, stride), 1) == 1
            ascending = jnp.bitwise_and(jnp.right_shift(places, level), 1) == 0
            smaller = key_list < partner_keys
            keep_own = (jnp.logical_not(upper_half) == smaller) == ascending
            keep_mine = jnp.any(jnp.logical_and(keep_own, places == position))
            payload = jnp.where(keep_mine, payload, partner)
            key_list = jnp.where(keep_own, key_list, partner_keys)
    for which_bit in range(low_bits):
        partner = part_swap(payload, which_bit)
        upper_side = jnp.bitwise_and(jnp.right_shift(head_index, which_bit), 1) == 1
        payload = jnp.where(
            upper_side,
            jnp.concatenate([partner, payload], axis=2),
            jnp.concatenate([payload, partner], axis=2),
        )
    pieces = []
    for offset_slot in range(slot_count):
        wanted = quarter * slot_count + offset_slot
        local_head = jnp.sum(jnp.arange(GROUP, dtype=jnp.int32) * (group_slots == wanted))
        pieces.append(lax.dynamic_slice_in_dim(payload, local_head * HEAD_DIM, HEAD_DIM, axis=2))
    pieces.append(payload[:, :, GROUP * HEAD_DIM :])
    return jnp.concatenate(pieces, axis=2)


def on_device(hidden, joined_weight, src_block, group_map, q_slot):
    head_count = lax.axis_size("head")
    per_group = head_count // KV_HEADS
    low_bits = per_group.bit_length() - 1
    sort_bits = KV_HEADS.bit_length() - 1
    slot_count = Q_HEADS // head_count
    head_index = lax.axis_index("head")
    position = head_index // per_group
    quarter = head_index % per_group
    rank_ids = jnp.arange(KV_HEADS, dtype=jnp.int32)
    rank_at = jnp.sum(rank_ids[None, :] * (src_block[None, :] == rank_ids[:, None]), axis=1)
    start_keys = lookup(group_map, rank_at)
    rank_here = jnp.sum(rank_ids * (group_map == position))
    group_slots = lax.dynamic_slice_in_dim(q_slot, rank_here * GROUP, GROUP)
    partial_value = jnp.einsum(
        "lrd,ldc->lrc", hidden, joined_weight, preferred_element_type=jnp.float32
    )
    summed = lax.psum_scatter(partial_value, "kdim", scatter_dimension=1, tiled=True)
    return regroup(
        summed,
        start_keys,
        position,
        quarter,
        head_index,
        group_slots,
        slot_count,
        low_bits,
        sort_bits,
        lambda piece, which_bit: from_partner(piece, "head", which_bit),
        lambda piece, which_bit: from_partner(piece, "head", which_bit),
    )


def solution(mesh):
    return jax.shard_map(
        on_device,
        mesh=mesh,
        in_specs=(P(None, None, "kdim"), P(None, "kdim", "head"), P(), P(), P()),
        out_specs=P(None, "kdim", "head"),
        check_vma=False,
    )
```

profile of v0, /device:TPU:0, one launch (start us, length us, event | category | flops | bytes accessed | tf_op | source)
XLA Modules:
  0.0 775.9 jit_solution(4166165227800450066)
XLA Ops:
  6.5 25.3 %fusion.14 = f32[3,1024,1280]{2,1,0:T(8,128)} fusion(bf16[3,1024,2048]{2,1,0:T(8,128)(2,1)} %param.5, bf16[3,2048,1280]{2,1,0:T(8,128)(2,1)} %param.6), kind=kOutput, calls=%fused_computation.71 | convolution fusion | flops 16106127360 | bytes 44040192 | tf_op jit(solution)/shard_map/lrd,ldc->lrc/dot_general | solution.py:85
  31.9 122.7 %reduce-scatter.2.cloned.1.call-done = f32[3,256,1280]{2,1,0:T(8,128)} async-done(((f32[3,1024,1280]{2,1,0:T(8,128)}), f32[3,256,1280]{2,1,0:T(8,128)}) %reduce-scatter.2.cloned.1.call-update) | async-done | bytes 3932176 | tf_op jit(solution)/shard_map/reduce_scatter | solution.py:88
  154.6 1.5 collective-permute-start
  156.3 0.2 select_reduce_fusion.5
  156.5 0.6 and_reduce_fusion
  157.2 84.4 %collective-permute-done = f32[3,256,1280]{2,1,0:T(8,128)} collective-permute-done((f32[3,256,1280]{2,1,0:T(8,128)}, f32[3,256,1280]{2,1,0:T(8,128)}, u32[]{:S(2)}, u32[]{:S(2)}) %collective-permute-start) | collective-permute-done | bytes 3932192 | tf_op jit(solution)/shard_map/ppermute | solution.py:19
  241.6 3.2 broadcast_select_fusion
  244.8 1.6 collective-permute-start.1
  246.6 0.6 and_reduce_fusion.1
  247.2 83.4 %collective-permute-done.1 = f32[3,256,1280]{2,1,0:T(8,128)S(1)} collective-permute-done((f32[3,256,1280]{2,1,0:T(8,128)S(1)}, f32[3,256,1280]{2,1,0:T(8,128)S(1)}, u32[]{:S(2)}, u32[]{:S(2)}) %collective-permute-start.1) | collective-permute-done | bytes 3932192 | tf_op jit(solution)/shard_map/ppermute | solution.py:19
  330.7 1.2 broadcast_select_fusion.1
  331.8 1.6 collective-permute-start.2
  333.6 0.6 and_reduce_fusion.2
  334.3 82.5 %collective-permute-done.2 = f32[3,256,1280]{2,1,0:T(8,128)S(1)} collective-permute-done((f32[3,256,1280]{2,1,0:T(8,128)S(1)}, f32[3,256,1280]{2,1,0:T(8,128)S(1)}, u32[]{:S(2)}, u32[]{:S(2)}) %collective-permute-start.2) | collective-permute-done | bytes 3932192 | tf_op jit(solution)/shard_map/ppermute | solution.py:19
  416.8 1.1 broadcast_select_fusion.2
  417.9 2.5 collective-permute-start.3
  420.6 0.6 and_reduce_fusion.3
  421.2 165.8 %collective-permute-done.3 = f32[3,256,1280]{2,1,0:T(8,128)S(1)} collective-permute-done((f32[3,256,1280]{2,1,0:T(8,128)S(1)}, f32[3,256,1280]{2,1,0:T(8,128)S(1)}, u32[]{:S(2)}, u32[]{:S(2)}) %collective-permute-start.3) | collective-permute-done | bytes 3932192 | tf_op jit(solution)/shard_map/ppermute | solution.py:19
  587.1 1.1 broadcast_select_fusion.3
  588.2 0.6 collective-permute-start.4
  588.8 0.2 select_reduce_fusion.1
  589.0 0.7 and_reduce_fusion.4
  589.7 84.3 %collective-permute-done.4 = f32[3,256,1280]{2,1,0:T(8,128)S(1)} collective-permute-done((f32[3,256,1280]{2,1,0:T(8,128)S(1)}, f32[3,256,1280]{2,1,0:T(8,128)S(1)}, u32[]{:S(2)}, u32[]{:S(2)}) %collective-permute-start.4) | collective-permute-done | bytes 3932192 | tf_op jit(solution)/shard_map/ppermute | solution.py:19
  674.0 3.1 broadcast_select_fusion.4
  677.1 1.8 collective-permute-start.5
  679.0 0.7 fusion
  680.3 0.9 fusion.8
  686.3 0.7 and_reduce_fusion.5
  687.0 75.6 %collective-permute-done.5 = f32[3,256,1280]{2,1,0:T(8,128)} collective-permute-done((f32[3,256,1280]{2,1,0:T(8,128)}, f32[3,256,1280]{2,1,0:T(8,128)}, u32[]{:S(2)}, u32[]{:S(2)}) %collective-permute-start.5) | collective-permute-done | bytes 3932192 | tf_op jit(solution)/shard_map/ppermute | solution.py:19
  762.6 3.2 broadcast_select_fusion.5
  766.2 1.9 copy-done
  768.1 0.9 slice_dynamic-update-slice_fusion
  (31 shorter events, 1.4 us)
Async XLA Ops:
  6.5 148.0 %reduce-scatter.2.cloned.1.call-start = ((), (), s32[]{:S(2)}) async-start(), calls=%async_computation.1 | async-start | bytes 19660800 | tf_op jit(solution)/shard_map/reduce_scatter | solution.py:88
  31.8 124.2 %copy-start.2 = (s32[8]{0:T(128)S(1)}, s32[8]{0:T(128)}, u32[]{:S(2)}) copy-start(s32[8]{0:T(128)} %param.7) | copy-start | bytes 100
  31.8 124.3 %copy-start.3 = (s32[8]{0:T(128)S(1)}, s32[8]{0:T(128)}, u32[]{:S(2)}) copy-start(s32[8]{0:T(128)} %param.8) | copy-start | bytes 100
  154.6 87.0 %collective-permute-start = (f32[3,256,1280]{2,1,0:T(8,128)}, f32[3,256,1280]{2,1,0:T(8,128)}, u32[]{:S(2)}, u32[]{:S(2)}) collective-permute-start(f32[3,256,1280]{2,1,0:T(8,128)} %reduce-scatter.2.cloned.1.call-done), channel_id=1, source_target_pairs={{0,4},{4,0},{8,12},{12,8},{16,20},{20,16},{24,28},{28,24},{1,5},{5... | collective-permute-start | bytes 11796488 | tf_op jit(solution)/shard_map/ppermute | solution.py:19
  244.8 85.9 %collective-permute-start.1 = (f32[3,256,1280]{2,1,0:T(8,128)S(1)}, f32[3,256,1280]{2,1,0:T(8,128)S(1)}, u32[]{:S(2)}, u32[]{:S(2)}) collective-permute-start(f32[3,256,1280]{2,1,0:T(8,128)S(1)} %broadcast_select_fusion), channel_id=1, source_target_pairs={{0,8},{8,0},{4,12},{12,4},{16,24},{24,16},{20,28},{28,20},{1,9},{9... | collective-permute-start | bytes 11796488 | tf_op jit(solution)/shard_map/ppermute | solution.py:19
  331.8 84.9 %collective-permute-start.2 = (f32[3,256,1280]{2,1,0:T(8,128)S(1)}, f32[3,256,1280]{2,1,0:T(8,128)S(1)}, u32[]{:S(2)}, u32[]{:S(2)}) collective-permute-start(f32[3,256,1280]{2,1,0:T(8,128)S(1)} %broadcast_select_fusion.1), channel_id=1, source_target_pairs={{0,4},{4,0},{8,12},{12,8},{16,20},{20,16},{24,28},{28,24},{1,5},{5... | collective-permute-start | bytes 11796488 | tf_op jit(solution)/shard_map/ppermute | solution.py:19
  417.9 169.2 %collective-permute-start.3 = (f32[3,256,1280]{2,1,0:T(8,128)S(1)}, f32[3,256,1280]{2,1,0:T(8,128)S(1)}, u32[]{:S(2)}, u32[]{:S(2)}) collective-permute-start(f32[3,256,1280]{2,1,0:T(8,128)S(1)} %broadcast_select_fusion.2), channel_id=1, source_target_pairs={{0,16},{16,0},{4,20},{20,4},{8,24},{24,8},{12,28},{28,12},{1,17},{... | collective-permute-start | bytes 11796488 | tf_op jit(solution)/shard_map/ppermute | solution.py:19
  588.2 85.8 %collective-permute-start.4 = (f32[3,256,1280]{2,1,0:T(8,128)S(1)}, f32[3,256,1280]{2,1,0:T(8,128)S(1)}, u32[]{:S(2)}, u32[]{:S(2)}) collective-permute-start(f32[3,256,1280]{2,1,0:T(8,128)S(1)} %broadcast_select_fusion.3), channel_id=1, source_target_pairs={{0,8},{8,0},{4,12},{12,4},{16,24},{24,16},{20,28},{28,20},{1,9},{9... | collective-permute-start | bytes 11796488 | tf_op jit(solution)/shard_map/ppermute | solution.py:19
  589.7 90.6 %copy-start.1 = (s32[64]{0:T(128)S(1)}, s32[64]{0:T(128)}, u32[]{:S(2)}) copy-start(s32[64]{0:T(128)} %param.9) | copy-start | bytes 772
  677.1 85.5 %collective-permute-start.5 = (f32[3,256,1280]{2,1,0:T(8,128)}, f32[3,256,1280]{2,1,0:T(8,128)}, u32[]{:S(2)}, u32[]{:S(2)}) collective-permute-start(f32[3,256,1280]{2,1,0:T(8,128)} %broadcast_select_fusion.4), channel_id=1, source_target_pairs={{0,4},{4,0},{8,12},{12,8},{16,20},{20,16},{24,28},{28,24},{1,5},{5... | collective-permute-start | bytes 11796488 | tf_op jit(solution)/shard_map/ppermute | solution.py:19
  766.2 1.9 copy-start
Sparse Core Ops, SparseCore 0:
  32.0 122.5 reduce-scatter.1
where the time goes:
time: 777 us; the launch traced here: 776 us
  waiting for transfers between devices  699 us (90%)
  matrix products  25.3 us (3%)
  other arithmetic  19.9 us (3%)
  between operations  19.2 us (2%)
  starting transfers between devices  9.56 us (1%)
    ppermute x6, waiting for transfers between devices, from_partner(): return lax.ppermute(block, axis, route)  576 us
    reduce_scatter x1, waiting for transfers between devices, on_device(): lax.psum_scatter(partial_value, 'kdim', scatter_dimension=1, tiled=True)  123 us
    dot_general x1, matrix products, on_device(): jnp.einsum('lrd,ldc->lrc', hidden, joined_weight, preferred_element_type=...  25.3 us
  transfers between devices with their start and end apart: 7, of which 7 were waited for; matrix products, arithmetic and copies ran while one was open for 1% of the time, Pallas kernels for 0%

commit v1 on v0

--- a/solution.py
+++ b/solution.py
@@ -68,6 +68,24 @@
     return jnp.concatenate(pieces, axis=2)
 
 
+def regroup_dense(payload, start_keys, group_slots, slot_count):
+    heads = lax.axis_size("head")
+    depth = payload.shape[1] // heads
+    ids = jnp.arange(heads, dtype=jnp.int32)
+    source = jnp.sum(ids[None, :] * (start_keys[None, :] == ids[:, None]), axis=1)
+    spread = lax.all_to_all(payload, "head", split_axis=1, concat_axis=1, tiled=True)
+    picked = jnp.concatenate(
+        [lax.dynamic_slice_in_dim(spread, source[d] * depth, depth, axis=1) for d in range(heads)], axis=1
+    )
+    payload = lax.all_to_all(picked, "head", split_axis=1, concat_axis=1, tiled=True)
+    pieces = []
+    for wanted in range(slot_count):
+        local_head = jnp.sum(jnp.arange(GROUP, dtype=jnp.int32) * (group_slots == wanted))
+        pieces.append(lax.dynamic_slice_in_dim(payload, local_head * HEAD_DIM, HEAD_DIM, axis=2))
+    pieces.append(payload[:, :, GROUP * HEAD_DIM :])
+    return jnp.concatenate(pieces, axis=2)
+
+
 def on_device(hidden, joined_weight, src_block, group_map, q_slot):
     head_count = lax.axis_size("head")
     per_group = head_count // KV_HEADS
@@ -86,6 +104,8 @@
         "lrd,ldc->lrc", hidden, joined_weight, preferred_element_type=jnp.float32
     )
     summed = lax.psum_scatter(partial_value, "kdim", scatter_dimension=1, tiled=True)
+    if head_count == KV_HEADS and summed.shape[1] % head_count == 0:
+        return regroup_dense(summed, start_keys, group_slots, slot_count)
     return regroup(
         summed,
         start_keys,

time: 777 us -> 441 us (0.57)
  waiting for transfers between devices: 699 us -> 340 us
  local copies, waits for them, and re-layouts: 3.14 us -> 38.1 us
  other arithmetic: 19.9 us -> 1.87 us
    ppermute x6 -> x0, waiting for transfers between devices: 576 us -> none  [from_partner(): return lax.ppermute(block, axis, route)]
    all_to_all x0 -> x2, waiting for transfers between devices: none -> 217 us  [the longest x1 110 us: regroup_dense(): lax.all_to_all(payload, 'head', split_axis=1, concat_axis=1, tiled=True)]
    unnamed x16 -> x21, local copies, waits for them, and re-layouts: 2.21 us -> 24.2 us
    select_n x11 -> x0, other arithmetic: 13 us -> none  [the longest x6 13 us: regroup(): payload = jnp.where(keep_mine, payload, partner)]
    all_to_all x0 -> x2, starting transfers between devices: none -> 10.4 us  [the longest x1 5.63 us: regroup_dense(): lax.all_to_all(payload, 'head', split_axis=1, concat_axis=1, tiled=True)]
    ppermute x6 -> x0, starting transfers between devices: 9.56 us -> none  [from_partner(): return lax.ppermute(block, axis, route)]
  transfers between devices with their start and end apart: 7 -> 3, of which waited for: 7 -> 3; matrix products, arithmetic and copies ran while one was open for 1% -> 1% of each run, Pallas kernels for 0% -> 0%
where the time goes in v1:
time: 441 us; the launch traced here: 440 us
  waiting for transfers between devices  340 us (77%)
  local copies, waits for them, and re-layouts  38.1 us (9%)
  matrix products  25.3 us (6%)
  between operations  24.1 us (5%)
  starting transfers between devices  10.4 us (2%)
    reduce_scatter x1, waiting for transfers between devices, on_device(): lax.psum_scatter(partial_value, 'kdim', scatter_dimension=1, tiled=True)  123 us
    all_to_all x1, waiting for transfers between devices, regroup_dense(): lax.all_to_all(payload, 'head', split_axis=1, concat_axis=1, tiled=True)  110 us
    all_to_all x1, waiting for transfers between devices, regroup_dense(): lax.all_to_all(picked, 'head', split_axis=1, concat_axis=1, tiled=True)  108 us
    dot_general x1, matrix products, on_device(): jnp.einsum('lrd,ldc->lrc', hidden, joined_weight, preferred_element_type=...  25.3 us
    unnamed x21, local copies, waits for them, and re-layouts  24.2 us
  transfers between devices with their start and end apart: 3, of which 3 were waited for; matrix products, arithmetic and copies ran while one was open for 1% of the time, Pallas kernels for 0%

profile of v1, /device:TPU:0, one launch (start us, length us, event | category | flops | bytes accessed | tf_op | source)
XLA Modules:
  0.0 440.0 jit_solution(17491024868623844181)
XLA Ops:
  6.5 25.3 %fusion.10 = f32[3,1024,1280]{2,1,0:T(8,128)} fusion(bf16[3,1024,2048]{2,1,0:T(8,128)(2,1)} %param.5, bf16[3,2048,1280]{2,1,0:T(8,128)(2,1)} %param.6), kind=kOutput, calls=%fused_computation.42 | convolution fusion | flops 16106127360 | bytes 44040192 | tf_op jit(solution)/shard_map/lrd,ldc->lrc/dot_general | solution.py:103
  31.8 0.0 reduce-scatter.2.cloned.1.call-update
  31.9 122.7 %reduce-scatter.2.cloned.1.call-done = f32[3,256,1280]{2,1,0:T(8,128)} async-done(((f32[3,1024,1280]{2,1,0:T(8,128)}), f32[3,256,1280]{2,1,0:T(8,128)}) %reduce-scatter.2.cloned.1.call-update) | async-done | bytes 3932176 | tf_op jit(solution)/shard_map/reduce_scatter | solution.py:106
  154.6 7.2 %copy.8 = f32[3,256,1280]{2,0,1:T(4,128)} copy(f32[3,256,1280]{2,1,0:T(8,128)} %reduce-scatter.2.cloned.1.call-done) | data formatting | bytes 7864320 | tf_op jit(solution)/shard_map/reduce_scatter | solution.py:106
  161.7 5.6 %all-to-all-start = ((f32[3,256,1280]{2,0,1:T(4,128)}), f32[3,256,1280]{2,0,1:T(4,128)}, u32[]{:S(2)}, u32[]{:S(2)}) async-start(f32[3,256,1280]{2,0,1:T(4,128)} %copy.8), calls=%async_computation.1 | async-start | bytes 10485760 | tf_op jit(solution)/shard_map/all_to_all | solution.py:76
  167.4 0.1 select_reduce_fusion.2
  167.5 0.2 select_reduce_fusion.1
  167.7 0.1 select_reduce_fusion
  167.8 0.7 fusion.9
  173.5 109.7 %all-to-all-done = f32[3,256,1280]{2,0,1:T(4,128)} async-done(((f32[3,256,1280]{2,0,1:T(4,128)}), f32[3,256,1280]{2,0,1:T(4,128)}, u32[]{:S(2)}, u32[]{:S(2)}) %all-to-all-start) | async-done | bytes 3932192 | tf_op jit(solution)/shard_map/all_to_all | solution.py:76
  283.1 2.1 dynamic-slice_dynamic-update-slice_fusion.7
  285.2 2.0 dynamic-slice_dynamic-update-slice_fusion.6
  287.2 2.0 dynamic-slice_dynamic-update-slice_fusion.5
  289.3 2.0 dynamic-slice_dynamic-update-slice_fusion.4
  291.3 2.1 dynamic-slice_dynamic-update-slice_fusion.3
  293.4 2.1 dynamic-slice_dynamic-update-slice_fusion.2
  295.5 2.1 dynamic-slice_dynamic-update-slice_fusion.1
  297.5 2.0 dynamic-slice_dynamic-update-slice_fusion
  299.6 4.8 %all-to-all-start.1 = ((f32[3,256,1280]{2,0,1:T(4,128)}), f32[3,256,1280]{2,0,1:T(4,128)}, u32[]{:S(2)}, u32[]{:S(2)}) async-start(f32[3,256,1280]{2,0,1:T(4,128)} %dynamic-slice_dynamic-update-slice_fusion), calls=%async_computation.2 | async-start | bytes 10485760 | tf_op jit(solution)/shard_map/all_to_all | solution.py:80
  304.4 0.6 fusion
  305.7 0.8 fusion.8
  311.5 107.8 %all-to-all-done.1 = f32[3,256,1280]{2,0,1:T(4,128)} async-done(((f32[3,256,1280]{2,0,1:T(4,128)}), f32[3,256,1280]{2,0,1:T(4,128)}, u32[]{:S(2)}, u32[]{:S(2)}) %all-to-all-start.1) | async-done | bytes 3932192 | tf_op jit(solution)/shard_map/all_to_all | solution.py:80
  419.3 1.1 dynamic-slice_dynamic-update-slice_fusion.15
  420.4 1.2 dynamic-slice_dynamic-update-slice_fusion.14
  421.6 1.2 dynamic-slice_dynamic-update-slice_fusion.13
  422.9 1.2 dynamic-slice_dynamic-update-slice_fusion.12
  424.1 1.2 dynamic-slice_dynamic-update-slice_fusion.11
  425.3 1.2 dynamic-slice_dynamic-update-slice_fusion.10
  426.6 1.2 dynamic-slice_dynamic-update-slice_fusion.9
  427.8 1.3 dynamic-slice_dynamic-update-slice_fusion.8
  429.1 1.5 slice_dynamic-update-slice_fusion
  430.6 2.6 copy.9
  (7 shorter events, 0.0 us)
Async XLA Ops:
  6.5 148.0 %reduce-scatter.2.cloned.1.call-start = ((), (), s32[]{:S(2)}) async-start(), calls=%async_computation.3 | async-start | bytes 19660800 | tf_op jit(solution)/shard_map/reduce_scatter | solution.py:106
  161.7 5.6 %copy-start.1 = (s32[8]{0:T(128)S(1)}, s32[8]{0:T(128)}, u32[]{:S(2)}) copy-start(s32[8]{0:T(128)} %param.7) | copy-start | bytes 100
  161.7 5.8 %copy-start.2 = (s32[8]{0:T(128)S(1)}, s32[8]{0:T(128)}, u32[]{:S(2)}) copy-start(s32[8]{0:T(128)} %param.8) | copy-start | bytes 100
  161.7 121.4 %all-to-all-start = ((f32[3,256,1280]{2,0,1:T(4,128)}), f32[3,256,1280]{2,0,1:T(4,128)}, u32[]{:S(2)}, u32[]{:S(2)}) async-start(f32[3,256,1280]{2,0,1:T(4,128)} %copy.8), calls=%async_computation.1 | async-start | bytes 10485760 | tf_op jit(solution)/shard_map/all_to_all | solution.py:76
  299.6 6.1 %copy-start = (s32[64]{0:T(128)S(1)}, s32[64]{0:T(128)}, u32[]{:S(2)}) copy-start(s32[64]{0:T(128)} %param.9) | copy-start | bytes 772
  299.6 119.7 %all-to-all-start.1 = ((f32[3,256,1280]{2,0,1:T(4,128)}), f32[3,256,1280]{2,0,1:T(4,128)}, u32[]{:S(2)}, u32[]{:S(2)}) async-start(f32[3,256,1280]{2,0,1:T(4,128)} %dynamic-slice_dynamic-update-slice_fusion), calls=%async_computation.2 | async-start | bytes 10485760 | tf_op jit(solution)/shard_map/all_to_all | solution.py:80
Sparse Core Ops, SparseCore 0:
  32.0 122.5 reduce-scatter.1

commit v2 on v0

--- a/solution.py
+++ b/solution.py
@@ -1,6 +1,9 @@
 import jax
 import jax.numpy as jnp
 from jax import lax
+import functools
+from jax.experimental import pallas as pl
+from jax.experimental.pallas import tpu as pltpu
 from jax.sharding import PartitionSpec as P
 
 HEAD_DIM = 128
@@ -68,6 +71,349 @@
     return jnp.concatenate(pieces, axis=2)
 
 
+SPLIT = 2
+TOP = 32767.0
+TINY = 1e-30
+CHUNK = 16
+
+
+def quantum(peak):
+    peak = jnp.maximum(peak, TINY)
+    return TOP / peak, peak * (1.0 / TOP)
+
+
+def spread_tile(tile, columns):
+    return jnp.concatenate([jnp.concatenate([tile] * (CHUNK // 8), axis=0)] * (columns // 128), axis=1)
+
+
+def fold_peak(value):
+    value = jnp.abs(value)
+    peak = value[:, :128]
+    for start in range(128, value.shape[1], 128):
+        peak = jnp.maximum(peak, value[:, start : start + 128])
+    return jnp.maximum(peak[:8], peak[8:])
+
+
+def code(value, inverse):
+    return jnp.round(value * inverse).astype(jnp.int32).astype(jnp.int16)
+
+
+def decode(coded, scale):
+    return coded.astype(jnp.int32).astype(jnp.float32) * scale
+
+
+def exchange_kernel(
+    layers, heads, stages, band, source_ref, hidden_ref, weight_ref, out_ref, scale_ref,
+    hbuf, wbuf, core_out, core_in, mine, hold, x_out, x_in, x_scale_out, x_scale_in,
+    spread_out, own_scale, bound_out, *rest,
+):
+    spread_in = rest[:stages]
+    load_sem, core_send, core_recv, x_send, x_recv, p_send, p_recv, s_send, s_recv, b_send, b_recv = rest[stages:]
+    columns = weight_ref.shape[2]
+    quarter = hidden_ref.shape[1] // 4
+    me = lax.axis_index("head")
+    k = lax.axis_index("kdim")
+    core, x = lax.rem(k, 2), lax.div(k, 2)
+    core_peer = x * 2 + 1 - core
+    x_peer = (1 - x) * 2 + core
+
+    def loads(layer):
+        slot = layer % 2
+        return (
+            pltpu.make_async_copy(hidden_ref.at[layer], hbuf.at[slot], load_sem.at[slot, 0]),
+            pltpu.make_async_copy(weight_ref.at[layer], wbuf.at[slot], load_sem.at[slot, 1]),
+        )
+
+    for layer in range(min(2, layers)):
+        for copy in loads(layer):
+            copy.start()
+
+    barrier = pltpu.get_barrier_semaphore()
+    for peer in (core_peer, x_peer):
+        pl.semaphore_signal(barrier, inc=1, device_id={"kdim": peer}, device_id_type=pl.DeviceIdType.MESH)
+
+    def greet(offset, carry):
+        pl.semaphore_signal(
+            barrier, inc=1, device_id={"head": lax.rem(me + offset, heads)}, device_id_type=pl.DeviceIdType.MESH
+        )
+        return carry
+
+    lax.fori_loop(1, heads, greet, 0)
+    pl.semaphore_wait(barrier, heads + 1)
+
+    def remote(source, target, send, recv, peer):
+        return pltpu.make_async_remote_copy(
+            src_ref=source, dst_ref=target, send_sem=send, recv_sem=recv,
+            device_id=peer, device_id_type=pl.DeviceIdType.MESH,
+        )
+
+    def core_copy(stage):
+        return remote(
+            core_out.at[stage], core_in.at[stage], core_send.at[stage], core_recv.at[stage], {"kdim": core_peer}
+        )
+
+    def x_copies(stage):
+        return (
+            remote(x_out.at[stage], x_in.at[stage], x_send.at[stage, 0], x_recv.at[stage, 0], {"kdim": x_peer}),
+            remote(
+                x_scale_out.at[stage], x_scale_in.at[stage], x_send.at[stage, 1], x_recv.at[stage, 1],
+                {"kdim": x_peer},
+            ),
+        )
+
+    def spread_copies(stage, peer, slot):
+        return (
+            remote(
+                spread_out.at[stage, peer], spread_in[stage].at[slot], p_send.at[stage, peer],
+                p_recv.at[stage, slot], {"head": peer},
+            ),
+            remote(
+                own_scale.at[stage], scale_ref.at[stage, slot], s_send.at[stage, peer],
+                s_recv.at[stage, slot], {"head": peer},
+            ),
+        )
+
+    def bound_copy(stage, peer, slot):
+        return remote(
+            bound_out.at[stage, peer], out_ref.at[stage, slot], b_send.at[stage, peer],
+            b_recv.at[stage, slot], {"head": peer},
+        )
+
+    def own_scale_copy(stage):
+        return pltpu.make_async_copy(own_scale.at[stage], scale_ref.at[stage, me], s_recv.at[stage, me])
+
+    def own_bound_copy(stage):
+        return pltpu.make_async_copy(bound_out.at[stage, me], out_ref.at[stage, me], b_recv.at[stage, me])
+
+    width = 256
+    tiles = columns // width
+    chunks = band // CHUNK
+
+    def product(stage, which_core, target):
+        slot, start = (stage // SPLIT) % 2, (stage % SPLIT) * band
+
+        def body(step, carry):
+            half, tile = lax.div(step, tiles), lax.rem(step, tiles)
+            row = pl.multiple_of((half * 2 + which_core) * quarter + start, band)
+            column = pl.multiple_of(tile * width, width)
+            target[half, :, pl.ds(column, width)] = jnp.dot(
+                hbuf[slot, pl.ds(row, band), :], wbuf[slot, :, pl.ds(column, width)],
+                preferred_element_type=jnp.float32,
+            )
+            return carry
+
+        lax.fori_loop(0, 2 * tiles, body, 0)
+
+    def rows_of(chunk):
+        return pl.ds(pl.multiple_of(chunk * CHUNK, CHUNK), CHUNK)
+
+    zero_peak = jnp.zeros((8, 128), jnp.float32)
+
+    def multiply(stage):
+        if stage % SPLIT == 0:
+            for copy in loads(stage // SPLIT):
+                copy.wait()
+        product(stage, 1 - core, core_out.at[stage])
+        core_copy(stage).start()
+        product(stage, core, mine)
+        layer = stage // SPLIT
+        if stage % SPLIT == SPLIT - 1 and layer + 2 < layers:
+            for copy in loads(layer + 2):
+                copy.start()
+        core_copy(stage).wait_recv()
+
+        def add(chunk, peak):
+            rows = rows_of(chunk)
+            hold[stage, rows, :] = mine[x, rows, :] + core_in[stage, x, rows, :]
+            other = mine[1 - x, rows, :] + core_in[stage, 1 - x, rows, :]
+            mine[1 - x, rows, :] = other
+            return jnp.maximum(peak, fold_peak(other))
+
+        inverse, scale = quantum(lax.fori_loop(0, chunks, add, zero_peak))
+        x_scale_out[stage] = scale
+        inverse = spread_tile(inverse, columns)
+
+        def pack(chunk, carry):
+            rows = rows_of(chunk)
+            x_out[stage, rows, :] = code(mine[1 - x, rows, :], inverse)
+            return carry
+
+        lax.fori_loop(0, chunks, pack, 0)
+        for copy in x_copies(stage):
+            copy.start()
+
+    def reduce(stage):
+        for copy in x_copies(stage):
+            copy.wait_recv()
+        arrived = spread_tile(x_scale_in[stage], columns)
+
+        def add(chunk, peak):
+            rows = rows_of(chunk)
+            total = hold[stage, rows, :] + decode(x_in[stage, rows, :], arrived)
+            hold[stage, rows, :] = total
+            return jnp.maximum(peak, fold_peak(total))
+
+        inverse, scale = quantum(lax.fori_loop(0, chunks, add, zero_peak))
+        own_scale[stage] = scale
+        inverse = spread_tile(inverse, columns)
+        per = chunks // heads
+
+        def pack(chunk, carry):
+            spread_out[stage, lax.div(chunk, per), rows_of(lax.rem(chunk, per)), :] = code(
+                hold[stage, rows_of(chunk), :], inverse
+            )
+            return carry
+
+        lax.fori_loop(0, chunks, pack, 0)
+
+        def send(offset, carry):
+            for copy in spread_copies(stage, lax.rem(me + offset, heads), me):
+                copy.start()
+            return carry
+
+        lax.fori_loop(1, heads, send, 0)
+        own_scale_copy(stage).start()
+        spread_in[stage][me] = spread_out[stage, me]
+
+    def forward(stage):
+        def arrive(offset, carry):
+            peer = lax.rem(me + offset, heads)
+            spread_copies(stage, peer, peer)[0].wait_recv()
+            return carry
+
+        lax.fori_loop(1, heads, arrive, 0)
+
+        def send(offset, carry):
+            peer = lax.rem(me + offset, heads)
+            bound_out[stage, peer] = spread_in[stage][source_ref[peer]]
+            bound_copy(stage, peer, me).start()
+            return carry
+
+        lax.fori_loop(1, heads, send, 0)
+        bound_out[stage, me] = spread_in[stage][source_ref[me]]
+        own_bound_copy(stage).start()
+
+    for step in range(stages + 4):
+        if step < stages:
+            multiply(step)
+        if 0 <= step - 1 < stages:
+            reduce(step - 1)
+        if 0 <= step - 2 < stages:
+            forward(step - 2)
+
+    def finish(stage, carry):
+        core_copy(stage).wait_send()
+        for copy in x_copies(stage):
+            copy.wait_send()
+
+        def one(offset, inner):
+            peer = lax.rem(me + offset, heads)
+            for copy in (
+                remote(
+                    spread_out.at[stage, peer], out_ref.at[stage, peer], p_send.at[stage, peer],
+                    p_recv.at[stage, peer], {"head": peer},
+                ),
+                remote(
+                    own_scale.at[stage], scale_ref.at[stage, peer], s_send.at[stage, peer],
+                    s_recv.at[stage, peer], {"head": peer},
+                ),
+                bound_copy(stage, peer, peer),
+            ):
+                copy.wait_send()
+            spread_scale = remote(
+                own_scale.at[stage], scale_ref.at[stage, peer], s_send.at[stage, peer],
+                s_recv.at[stage, peer], {"head": peer},
+            )
+            spread_scale.wait_recv()
+            bound_copy(stage, peer, peer).wait_recv()
+            return inner
+
+        lax.fori_loop(1, heads, one, 0)
+        own_scale_copy(stage).wait()
+        own_bound_copy(stage).wait()
+        return carry
+
+    lax.fori_loop(0, stages, finish, 0)
+
+
+def place_kernel(where_ref, coded_ref, scale_ref, out_ref):
+    rows = coded_ref.shape[1]
+    scale = jnp.concatenate([scale_ref[0, 0]] * (rows // 8), axis=0)
+    for slot in range(GROUP):
+        start = pl.multiple_of(where_ref[1 + slot] * HEAD_DIM, HEAD_DIM)
+        out_ref[0, :, slot * HEAD_DIM : (slot + 1) * HEAD_DIM] = decode(
+            coded_ref[0, :, pl.ds(start, HEAD_DIM)], scale
+        )
+    for start in range(GROUP * HEAD_DIM, coded_ref.shape[2], HEAD_DIM):
+        out_ref[0, :, start : start + HEAD_DIM] = decode(coded_ref[0, :, start : start + HEAD_DIM], scale)
+
+
+def fused(hidden, joined_weight, start_keys, head_index, group_slots):
+    layers, rows, depth = hidden.shape
+    columns = joined_weight.shape[2]
+    heads = lax.axis_size("head")
+    stages = layers * SPLIT
+    band = rows // 4 // SPLIT
+    piece = band // heads
+    ids = jnp.arange(heads, dtype=jnp.int32)
+    source = jnp.sum(ids[None, :] * (start_keys[None, :] == ids[:, None]), axis=1).astype(jnp.int32)
+    f32, i16 = jnp.float32, jnp.int16
+    hbm = pl.BlockSpec(memory_space=pl.ANY)
+    dma = pltpu.SemaphoreType.DMA
+    coded, scales = pl.pallas_call(
+        functools.partial(exchange_kernel, layers, heads, stages, band),
+        out_shape=[
+            jax.ShapeDtypeStruct((stages, heads, piece, columns), i16),
+            jax.ShapeDtypeStruct((stages, heads, 8, 128), f32),
+        ],
+        in_specs=[pl.BlockSpec(memory_space=pltpu.SMEM), hbm, hbm],
+        out_specs=[hbm, hbm],
+        scratch_shapes=[
+            pltpu.VMEM((2, rows, depth), hidden.dtype),
+            pltpu.VMEM((2, depth, columns), joined_weight.dtype),
+            pltpu.VMEM((stages, 2, band, columns), f32),
+            pltpu.VMEM((stages, 2, band, columns), f32),
+            pltpu.VMEM((2, band, columns), f32),
+            pltpu.VMEM((stages, band, columns), f32),
+            pltpu.VMEM((stages, band, columns), i16),
+            pltpu.VMEM((stages, band, columns), i16),
+            pltpu.VMEM((stages, 8, 128), f32),
+            pltpu.VMEM((stages, 8, 128), f32),
+            pltpu.VMEM((stages, heads, piece, columns), i16),
+            pltpu.VMEM((stages, 8, 128), f32),
+            pltpu.VMEM((stages, heads, piece, columns), i16),
+        ]
+        + [pltpu.VMEM((heads, piece, columns), i16) for _ in range(stages)]
+        + [dma((2, 2)), dma((stages,)), dma((stages,)), dma((stages, 2)), dma((stages, 2))]
+        + [dma((stages, heads)) for _ in range(6)],
+        compiler_params=pltpu.CompilerParams(
+            collective_id=0, has_side_effects=True, vmem_limit_bytes=58 * 2**20
+        ),
+        cost_estimate=pl.CostEstimate(
+            flops=2 * layers * rows * depth * columns, transcendentals=0,
+            bytes_accessed=2 * layers * depth * (rows + columns),
+        ),
+    )(source, hidden, joined_weight)
+    slots = jnp.arange(GROUP, dtype=jnp.int32)
+    local = jnp.sum(slots[None, :] * (group_slots[None, :] == slots[:, None]), axis=1)
+    mine = jnp.sum(source * (ids == head_index))
+    where_at = jnp.concatenate([mine[None], local]).astype(jnp.int32)
+    out = pl.pallas_call(
+        place_kernel,
+        grid_spec=pltpu.PrefetchScalarGridSpec(
+            num_scalar_prefetch=1,
+            grid=(stages,),
+            in_specs=[
+                pl.BlockSpec((1, band, columns), lambda s, where_ref: (s, 0, 0)),
+                pl.BlockSpec((1, 1, 8, 128), lambda s, where_ref: (s, where_ref[0], 0, 0)),
+            ],
+            out_specs=pl.BlockSpec((1, band, columns), lambda s, where_ref: (s, 0, 0)),
+        ),
+        out_shape=jax.ShapeDtypeStruct((stages, band, columns), f32),
+    )(where_at, coded.reshape(stages, band, columns), scales)
+    return out.reshape(layers, rows // 4, columns)
+
+
 def on_device(hidden, joined_weight, src_block, group_map, q_slot):
     head_count = lax.axis_size("head")
     per_group = head_count // KV_HEADS
@@ -82,6 +428,9 @@
     start_keys = lookup(group_map, rank_at)
     rank_here = jnp.sum(rank_ids * (group_map == position))
     group_slots = lax.dynamic_slice_in_dim(q_slot, rank_here * GROUP, GROUP)
+    heads_fit = head_count == KV_HEADS and joined_weight.shape[2] == (GROUP + 2) * HEAD_DIM
+    if heads_fit and lax.axis_size("kdim") == 4 and hidden.shape[1] % (4 * SPLIT * CHUNK * head_count) == 0:
+        return fused(hidden, joined_weight, start_keys, head_index, group_slots)
     partial_value = jnp.einsum(
         "lrd,ldc->lrc", hidden, joined_weight, preferred_element_type=jnp.float32
     )

time: 777 us -> 128 us (0.16)
  waiting for transfers between devices: 699 us -> 0 us
  Pallas kernels: 0 us -> 122 us
  matrix products: 25.3 us -> 0 us
  between operations: 19.2 us -> 0.72 us
  other arithmetic: 19.9 us -> 4.46 us
  starting transfers between devices: 9.56 us -> 0 us
    ppermute x6 -> x0, waiting for transfers between devices: 576 us -> none  [from_partner(): return lax.ppermute(block, axis, route)]
    reduce_scatter x1 -> x0, waiting for transfers between devices: 123 us -> none  [on_device(): lax.psum_scatter(partial_value, 'kdim', scatter_dimension=1, tiled=True)]
    pallas_call x0 -> x2, Pallas kernels: none -> 122 us  [the longest x1 116 us: fused(): pl.pallas_call(functools.partial(exchange_kernel, layers, heads, stages,...]
    dot_general x1 -> x0, matrix products: 25.3 us -> none  [on_device(): jnp.einsum('lrd,ldc->lrc', hidden, joined_weight, preferred_element_type=...]
    select_n x11 -> x0, other arithmetic: 13 us -> none  [the longest x6 13 us: regroup(): payload = jnp.where(keep_mine, payload, partner)]
    ppermute x6 -> x0, starting transfers between devices: 9.56 us -> none  [from_partner(): return lax.ppermute(block, axis, route)]
  transfers between devices with their start and end apart: 7 -> 0, of which waited for: 7 -> 0; matrix products, arithmetic and copies ran while one was open for 1% -> 0% of each run, Pallas kernels for 0% -> 0%
where the time goes in v2:
time: 128 us
  Pallas kernels  122 us (95%)
  other arithmetic  4.46 us (3%)
    pallas_call x1, Pallas kernels, fused(): pl.pallas_call(functools.partial(exchange_kernel, layers, heads, stages,...  116 us
    pallas_call x1, Pallas kernels, fused(): pl.pallas_call(place_kernel, grid_spec=pltpu.PrefetchScalarGridSpec(num_s...  5.75 us

profile of v2, /device:TPU:0, one launch (start us, length us, event | category | flops | bytes accessed | tf_op | source)
XLA Modules:
  0.0 127.6 jit_solution(16384149735432812269)
XLA Ops:
  0.0 0.8 select_reduce_fusion.3
  0.8 0.8 select_reduce_fusion.2
  1.6 0.1 select_reduce_fusion.1.source_ref
  1.7 0.0 copy-start
  1.7 1.4 %fusion = (s32[]{:T(128)}, s32[]{:T(128)}) fusion(s32[8]{0:T(128)S(1)} %select_reduce_fusion.1.source_ref, s32[]{:T(128)S(6)} %axis_index.15, s32[8]{0:T(128)} %param.8), kind=kLoop, calls=%fused_computation.10 | loop fusion | flops 46 | bytes 76 | tf_op jit(solution)/shard_map/reduce_sum | solution.py:399
  3.8 0.7 dynamic_slice.3
  4.5 0.1 select_reduce_fusion
  4.7 1.2 pad_add_fusion.where_ref
  5.9 0.0 copy-done
  5.9 116.0 %shard_map.55 = (s16[6,8,16,1280]{3,2,1,0:T(8,128)(2,1)}, f32[6,8,8,128]{3,2,1,0:T(8,128)}) custom-call(s32[8]{0:T(128)} %copy-done, bf16[3,1024,2048]{2,1,0:T(8,128)(2,1)} %hidden_ref.1, bf16[3,2048,1280]{2,1,0:T(8,128)(2,1)} %weight_ref.1), custom_call_target="tpu_custom_call" | custom-call | flops 16106127360 | bytes 28311552 | tf_op jit(solution)/shard_map/pallas_call | solution.py:363
  121.9 5.8 %shard_map.56 = f32[6,128,1280]{2,1,0:T(8,128)} custom-call(s32[9]{0:T(128)} %pad_add_fusion.where_ref, s16[6,128,1280]{2,1,0:T(8,128)(2,1)} %bitcast.3, f32[6,8,8,128]{3,2,1,0:T(8,128)} %get-tuple-element.8.scale_ref), custom_call_target="tpu_custom_call" | custom-call | tf_op jit(solution)/shard_map/pallas_call | solution.py:401
Async XLA Ops:
  1.7 4.2 %copy-start = (s32[8]{0:T(128)}, s32[8]{0:T(128)S(1)}, u32[]{:S(2)}) copy-start(s32[8]{0:T(128)S(1)} %select_reduce_fusion.1.source_ref) | copy-start | bytes 100

commit v3 on v2

--- a/solution.py
+++ b/solution.py
@@ -103,7 +103,7 @@
 
 
 def exchange_kernel(
-    layers, heads, stages, band, source_ref, hidden_ref, weight_ref, out_ref, scale_ref,
+    layers, heads, stages, band, source_block_ref, group_map_ref, hidden_ref, weight_ref, out_ref, scale_ref,
     hbuf, wbuf, core_out, core_in, mine, hold, x_out, x_in, x_scale_out, x_scale_in,
     spread_out, own_scale, bound_out, *rest,
 ):
@@ -119,14 +119,29 @@
 
     def loads(layer):
         slot = layer % 2
-        return (
-            pltpu.make_async_copy(hidden_ref.at[layer], hbuf.at[slot], load_sem.at[slot, 0]),
-            pltpu.make_async_copy(weight_ref.at[layer], wbuf.at[slot], load_sem.at[slot, 1]),
-        )
-
-    for layer in range(min(2, layers)):
-        for copy in loads(layer):
-            copy.start()
+        rows = [
+            [
+                pltpu.make_async_copy(
+                    hidden_ref.at[layer, pl.ds(which * quarter + part * band, band)],
+                    hbuf.at[slot, part, pl.ds((which % 2 * 2 + which // 2) * band, band)],
+                    load_sem.at[slot, part * 4 + which],
+                )
+                for which in range(4)
+            ]
+            for part in range(SPLIT)
+        ]
+        weight = pltpu.make_async_copy(weight_ref.at[layer], wbuf.at[slot], load_sem.at[slot, SPLIT * 4])
+        return rows, weight
+
+    def start_loads(layer):
+        rows, weight = loads(layer)
+        for part in range(SPLIT):
+            for copy in rows[part]:
+                copy.start()
+            if part == 0:
+                weight.start()
+
+    start_loads(0)
 
     barrier = pltpu.get_barrier_semaphore()
     for peer in (core_peer, x_peer):
@@ -140,6 +155,12 @@
 
     lax.fori_loop(1, heads, greet, 0)
     pl.semaphore_wait(barrier, heads + 1)
+
+    def source_of(head):
+        found = 0
+        for rank in range(heads):
+            found = found + jnp.where(group_map_ref[rank] == head, source_block_ref[rank], 0)
+        return found
 
     def remote(source, target, send, recv, peer):
         return pltpu.make_async_remote_copy(
@@ -190,19 +211,20 @@
     chunks = band // CHUNK
 
     def product(stage, which_core, target):
-        slot, start = (stage // SPLIT) % 2, (stage % SPLIT) * band
-
-        def body(step, carry):
-            half, tile = lax.div(step, tiles), lax.rem(step, tiles)
-            row = pl.multiple_of((half * 2 + which_core) * quarter + start, band)
+        slot, part = (stage // SPLIT) % 2, stage % SPLIT
+        row = pl.multiple_of(which_core * 2 * band, 2 * band)
+
+        def body(tile, carry):
             column = pl.multiple_of(tile * width, width)
-            target[half, :, pl.ds(column, width)] = jnp.dot(
-                hbuf[slot, pl.ds(row, band), :], wbuf[slot, :, pl.ds(column, width)],
+            both = jnp.dot(
+                hbuf[slot, part, pl.ds(row, 2 * band), :], wbuf[slot, :, pl.ds(column, width)],
                 preferred_element_type=jnp.float32,
             )
-            return carry
-
-        lax.fori_loop(0, 2 * tiles, body, 0)
+            target[0, :, pl.ds(column, width)] = both[:band]
+            target[1, :, pl.ds(column, width)] = both[band:]
+            return carry
+
+        lax.fori_loop(0, tiles, body, 0)
 
     def rows_of(chunk):
         return pl.ds(pl.multiple_of(chunk * CHUNK, CHUNK), CHUNK)
@@ -210,16 +232,19 @@
     zero_peak = jnp.zeros((8, 128), jnp.float32)
 
     def multiply(stage):
+        rows, weight = loads(stage // SPLIT)
+        for copy in rows[stage % SPLIT]:
+            copy.wait()
         if stage % SPLIT == 0:
-            for copy in loads(stage // SPLIT):
-                copy.wait()
+            weight.wait()
+        if stage == 0 and layers > 1:
+            start_loads(1)
         product(stage, 1 - core, core_out.at[stage])
         core_copy(stage).start()
         product(stage, core, mine)
         layer = stage // SPLIT
         if stage % SPLIT == SPLIT - 1 and layer + 2 < layers:
-            for copy in loads(layer + 2):
-                copy.start()
+            start_loads(layer + 2)
         core_copy(stage).wait_recv()
 
         def add(chunk, peak):
@@ -253,9 +278,10 @@
             hold[stage, rows, :] = total
             return jnp.maximum(peak, fold_peak(total))
 
-        inverse, scale = quantum(lax.fori_loop(0, chunks, add, zero_peak))
+        peak = lax.fori_loop(0, chunks, add, zero_peak)
+        inverse, scale = quantum(jnp.max(peak, axis=0, keepdims=True))
         own_scale[stage] = scale
-        inverse = spread_tile(inverse, columns)
+        inverse = jnp.concatenate([inverse] * (columns // 128), axis=1)
         per = chunks // heads
 
         def pack(chunk, carry):
@@ -285,12 +311,12 @@
 
         def send(offset, carry):
             peer = lax.rem(me + offset, heads)
-            bound_out[stage, peer] = spread_in[stage][source_ref[peer]]
+            bound_out[stage, peer] = spread_in[stage][source_of(peer)]
             bound_copy(stage, peer, me).start()
             return carry
 
         lax.fori_loop(1, heads, send, 0)
-        bound_out[stage, me] = spread_in[stage][source_ref[me]]
+        bound_out[stage, me] = spread_in[stage][source_of(me)]
         own_bound_copy(stage).start()
 
     for step in range(stages + 4):
@@ -336,27 +362,36 @@
     lax.fori_loop(0, stages, finish, 0)
 
 
-def place_kernel(where_ref, coded_ref, scale_ref, out_ref):
-    rows = coded_ref.shape[1]
-    scale = jnp.concatenate([scale_ref[0, 0]] * (rows // 8), axis=0)
+def place_kernel(source_block_ref, group_map_ref, q_slot_ref, coded_ref, scale_ref, out_ref):
+    me = lax.axis_index("head")
+    rank = 0
+    for other in range(KV_HEADS):
+        rank = rank + jnp.where(group_map_ref[other] == me, other, 0)
+    mine = source_block_ref[rank]
+    scales = [scale_ref[part, mine] for part in range(SPLIT)]
     for slot in range(GROUP):
-        start = pl.multiple_of(where_ref[1 + slot] * HEAD_DIM, HEAD_DIM)
-        out_ref[0, :, slot * HEAD_DIM : (slot + 1) * HEAD_DIM] = decode(
-            coded_ref[0, :, pl.ds(start, HEAD_DIM)], scale
-        )
+        local = 0
+        for member in range(GROUP):
+            local = local + jnp.where(q_slot_ref[rank * GROUP + member] == slot, member, 0)
+        start = pl.multiple_of(local * HEAD_DIM, HEAD_DIM)
+        for part in range(SPLIT):
+            out_ref[part, :, slot * HEAD_DIM : (slot + 1) * HEAD_DIM] = decode(
+                coded_ref[part, :, pl.ds(start, HEAD_DIM)], scales[part]
+            )
     for start in range(GROUP * HEAD_DIM, coded_ref.shape[2], HEAD_DIM):
-        out_ref[0, :, start : start + HEAD_DIM] = decode(coded_ref[0, :, start : start + HEAD_DIM], scale)
-
-
-def fused(hidden, joined_weight, start_keys, head_index, group_slots):
+        for part in range(SPLIT):
+            out_ref[part, :, start : start + HEAD_DIM] = decode(
+                coded_ref[part, :, start : start + HEAD_DIM], scales[part]
+            )
+
+
+def fused(hidden, joined_weight, src_block, group_map, q_slot):
     layers, rows, depth = hidden.shape
     columns = joined_weight.shape[2]
     heads = lax.axis_size("head")
     stages = layers * SPLIT
     band = rows // 4 // SPLIT
     piece = band // heads
-    ids = jnp.arange(heads, dtype=jnp.int32)
-    source = jnp.sum(ids[None, :] * (start_keys[None, :] == ids[:, None]), axis=1).astype(jnp.int32)
     f32, i16 = jnp.float32, jnp.int16
     hbm = pl.BlockSpec(memory_space=pl.ANY)
     dma = pltpu.SemaphoreType.DMA
@@ -364,12 +399,12 @@
         functools.partial(exchange_kernel, layers, heads, stages, band),
         out_shape=[
             jax.ShapeDtypeStruct((stages, heads, piece, columns), i16),
-            jax.ShapeDtypeStruct((stages, heads, 8, 128), f32),
+            jax.ShapeDtypeStruct((stages, heads, 1, 128), f32),
         ],
-        in_specs=[pl.BlockSpec(memory_space=pltpu.SMEM), hbm, hbm],
+        in_specs=[pl.BlockSpec(memory_space=pltpu.SMEM)] * 2 + [hbm, hbm],
         out_specs=[hbm, hbm],
         scratch_shapes=[
-            pltpu.VMEM((2, rows, depth), hidden.dtype),
+            pltpu.VMEM((2, SPLIT, 4 * band, depth), hidden.dtype),
             pltpu.VMEM((2, depth, columns), joined_weight.dtype),
             pltpu.VMEM((stages, 2, band, columns), f32),
             pltpu.VMEM((stages, 2, band, columns), f32),
@@ -380,11 +415,11 @@
             pltpu.VMEM((stages, 8, 128), f32),
             pltpu.VMEM((stages, 8, 128), f32),
             pltpu.VMEM((stages, heads, piece, columns), i16),
-            pltpu.VMEM((stages, 8, 128), f32),
+            pltpu.VMEM((stages, 1, 128), f32),
             pltpu.VMEM((stages, heads, piece, columns), i16),
         ]
         + [pltpu.VMEM((heads, piece, columns), i16) for _ in range(stages)]
-        + [dma((2, 2)), dma((stages,)), dma((stages,)), dma((stages, 2)), dma((stages, 2))]
+        + [dma((2, SPLIT * 4 + 1)), dma((stages,)), dma((stages,)), dma((stages, 2)), dma((stages, 2))]
         + [dma((stages, heads)) for _ in range(6)],
         compiler_params=pltpu.CompilerParams(
             collective_id=0, has_side_effects=True, vmem_limit_bytes=58 * 2**20
@@ -393,24 +428,20 @@
             flops=2 * layers * rows * depth * columns, transcendentals=0,
             bytes_accessed=2 * layers * depth * (rows + columns),
         ),
-    )(source, hidden, joined_weight)
-    slots = jnp.arange(GROUP, dtype=jnp.int32)
-    local = jnp.sum(slots[None, :] * (group_slots[None, :] == slots[:, None]), axis=1)
-    mine = jnp.sum(source * (ids == head_index))
-    where_at = jnp.concatenate([mine[None], local]).astype(jnp.int32)
+    )(src_block, group_map, hidden, joined_weight)
     out = pl.pallas_call(
         place_kernel,
         grid_spec=pltpu.PrefetchScalarGridSpec(
-            num_scalar_prefetch=1,
-            grid=(stages,),
+            num_scalar_prefetch=3,
+            grid=(layers,),
             in_specs=[
-                pl.BlockSpec((1, band, columns), lambda s, where_ref: (s, 0, 0)),
-                pl.BlockSpec((1, 1, 8, 128), lambda s, where_ref: (s, where_ref[0], 0, 0)),
+                pl.BlockSpec((SPLIT, band, columns), lambda s, *tables: (s, 0, 0)),
+                pl.BlockSpec((SPLIT, heads, 1, 128), lambda s, *tables: (s, 0, 0, 0)),
             ],
-            out_specs=pl.BlockSpec((1, band, columns), lambda s, where_ref: (s, 0, 0)),
+            out_specs=pl.BlockSpec((SPLIT, band, columns), lambda s, *tables: (s, 0, 0)),
         ),
         out_shape=jax.ShapeDtypeStruct((stages, band, columns), f32),
-    )(where_at, coded.reshape(stages, band, columns), scales)
+    )(src_block, group_map, q_slot, coded.reshape(stages, band, columns), scales)
     return out.reshape(layers, rows // 4, columns)
 
 
@@ -430,7 +461,7 @@
     group_slots = lax.dynamic_slice_in_dim(q_slot, rank_here * GROUP, GROUP)
     heads_fit = head_count == KV_HEADS and joined_weight.shape[2] == (GROUP + 2) * HEAD_DIM
     if heads_fit and lax.axis_size("kdim") == 4 and hidden.shape[1] % (4 * SPLIT * CHUNK * head_count) == 0:
-        return fused(hidden, joined_weight, start_keys, head_index, group_slots)
+        return fused(hidden, joined_weight, src_block, group_map, q_slot)
     partial_value = jnp.einsum(
         "lrd,ldc->lrc", hidden, joined_weight, preferred_element_type=jnp.float32
     )

time: 128 us -> 116 us (0.906)
  Pallas kernels: 122 us -> 116 us
  other arithmetic: 4.46 us -> 0 us
    pallas_call x1, Pallas kernels: 116 us -> 111 us  [fused(): pl.pallas_call(functools.partial(exchange_kernel, layers, heads, stages,...]
    reduce_sum x5 -> x0, other arithmetic: 3.22 us -> none  [the longest x1 1.38 us: fused(): mine = jnp.sum(source * (ids == head_index))]
where the time goes in v3:
time: 116 us
  Pallas kernels  116 us (100%)
    pallas_call x1, Pallas kernels, fused(): pl.pallas_call(functools.partial(exchange_kernel, layers, heads, stages,...  111 us
    pallas_call x1, Pallas kernels, fused(): pl.pallas_call(place_kernel, grid_spec=pltpu.PrefetchScalarGridSpec(num_s...  4.72 us

profile of v3, /device:TPU:0, one launch (start us, length us, event | category | flops | bytes accessed | tf_op | source)
XLA Modules:
  0.0 115.8 jit_solution(14410179918227933493)
XLA Ops:
  0.0 111.1 %shard_map.55 = (s16[6,8,16,1280]{3,2,1,0:T(8,128)(2,1)}, f32[6,8,1,128]{3,2,1,0:T(1,128)}) custom-call(s32[8]{0:T(128)} %source_block_ref.3, s32[8]{0:T(128)} %group_map_ref.3, bf16[3,1024,2048]{2,1,0:T(8,128)(2,1)} %hidden_ref.1, bf16[3,2048,1280]{2,1,0:T(8,128)(2,1)} %weight_ref.1), custom_call_target="tpu_custom_call" | custom-call | flops 16106127360 | bytes 28311552 | tf_op jit(solution)/shard_map/pallas_call | solution.py:398
  111.1 4.7 %shard_map.56 = f32[6,128,1280]{2,1,0:T(8,128)} custom-call(s32[8]{0:T(128)} %source_block_ref.3, s32[8]{0:T(128)} %group_map_ref.3, s32[64]{0:T(128)} %q_slot_ref.1, s16[6,128,1280]{2,1,0:T(8,128)(2,1)} %bitcast.2, f32[6,8,1,128]{3,2,1,0:T(1,128)} %get-tuple-element.8.scale_ref), custom_call_target="tpu_custom_call" | custom-call | tf_op jit(solution)/shard_map/pallas_call | solution.py:432

commit v4 on v3

--- a/solution.py
+++ b/solution.py
@@ -156,6 +156,9 @@
     lax.fori_loop(1, heads, greet, 0)
     pl.semaphore_wait(barrier, heads + 1)
 
+    def far_first(turn):
+        return lax.rem(me + heads // 2 + lax.div(turn, 2) * (1 - 2 * lax.rem(turn, 2)), heads)
+
     def source_of(head):
         found = 0
         for rank in range(heads):
@@ -293,7 +296,7 @@
         lax.fori_loop(0, chunks, pack, 0)
 
         def send(offset, carry):
-            for copy in spread_copies(stage, lax.rem(me + offset, heads), me):
+            for copy in spread_copies(stage, far_first(offset), me):
                 copy.start()
             return carry
 
@@ -310,7 +313,7 @@
         lax.fori_loop(1, heads, arrive, 0)
 
         def send(offset, carry):
-            peer = lax.rem(me + offset, heads)
+            peer = far_first(offset)
             bound_out[stage, peer] = spread_in[stage][source_of(peer)]
             bound_copy(stage, peer, me).start()
             return carry
@@ -324,8 +327,8 @@
             multiply(step)
         if 0 <= step - 1 < stages:
             reduce(step - 1)
-        if 0 <= step - 2 < stages:
-            forward(step - 2)
+        if 0 <= step - 3 < stages:
+            forward(step - 3)
 
     def finish(stage, carry):
         core_copy(stage).wait_send()

time: 116 us -> 118 us (1.017)
  Pallas kernels: 116 us -> 118 us
    pallas_call x1, Pallas kernels: 111 us -> 113 us  [fused(): pl.pallas_call(functools.partial(exchange_kernel, layers, heads, stages,...]
where the time goes in v4:
time: 118 us
  Pallas kernels  118 us (100%)
    pallas_call x1, Pallas kernels, fused(): pl.pallas_call(functools.partial(exchange_kernel, layers, heads, stages,...  113 us
    pallas_call x1, Pallas kernels, fused(): pl.pallas_call(place_kernel, grid_spec=pltpu.PrefetchScalarGridSpec(num_s...  4.72 us

profile of v4, /device:TPU:0, one launch (start us, length us, event | category | flops | bytes accessed | tf_op | source)
XLA Modules:
  0.0 117.6 jit_solution(17548296832186736727)
XLA Ops:
  0.0 112.8 %shard_map.55 = (s16[6,8,16,1280]{3,2,1,0:T(8,128)(2,1)}, f32[6,8,1,128]{3,2,1,0:T(1,128)}) custom-call(s32[8]{0:T(128)} %source_block_ref.3, s32[8]{0:T(128)} %group_map_ref.3, bf16[3,1024,2048]{2,1,0:T(8,128)(2,1)} %hidden_ref.1, bf16[3,2048,1280]{2,1,0:T(8,128)(2,1)} %weight_ref.1), custom_call_target="tpu_custom_call" | custom-call | flops 16106127360 | bytes 28311552 | tf_op jit(solution)/shard_map/pallas_call | solution.py:401
  112.8 4.7 %shard_map.56 = f32[6,128,1280]{2,1,0:T(8,128)} custom-call(s32[8]{0:T(128)} %source_block_ref.3, s32[8]{0:T(128)} %group_map_ref.3, s32[64]{0:T(128)} %q_slot_ref.1, s16[6,128,1280]{2,1,0:T(8,128)(2,1)} %bitcast.2, f32[6,8,1,128]{3,2,1,0:T(1,128)} %get-tuple-element.8.scale_ref), custom_call_target="tpu_custom_call" | custom-call | tf_op jit(solution)/shard_map/pallas_call | solution.py:435
